TPU v7x, 128 devices: a whole 4x4x4 slice. The times are simulated.
128 devices in a mesh: dp: 8 (over y, core), group: 16 (over x, z).
Axes of the slice: x: 4, y: 4, z: 4, core: 2. Of those that a mesh axis runs over, the one named last changes fastest.
Arguments:
- tile_maps: bfloat16 [1024, 16, 16, 384], P(('dp', 'group')), may hold values from -45 to 45
- positions: int32 [2, 1024], P(None, ('dp', 'group')), may hold values from 0 to 511
- counts: int32 [8], P('dp'), may hold values from 1 to 128, as said below
- routing: int32 [8, 16, 8], P(None, 'group'), may hold values from -1 to 31, as said below
- depth_kernel: float32 [49, 384], replicated, may hold values from -0.875 to 0.875
- depth_bias: float32 [384], replicated, may hold values from -3 to 3
- norm_gain: float32 [384], replicated, may hold values from 0.25 to 1.75
- norm_shift: float32 [384], replicated, may hold values from -2 to 2
- expand_weight: bfloat16 [384, 1536], replicated, may hold values from -0.3125 to 0.3125
- expand_bias: float32 [1536], replicated, may hold values from -1.15 to -0.75
- reduce_weight: bfloat16 [1536, 384], replicated, may hold values from -0.15625 to 0.15625
- reduce_bias: float32 [384], replicated, may hold values from -2 to 2
- layer_scale: float32 [384], replicated, may hold values from 0.3 to 1.5
- head_weight: bfloat16 [384, 768], replicated, may hold values from -0.3125 to 0.3125
- slide_taps: float32 [7, 768], replicated, may hold values from -2.5 to 2.5
- slide_weight: bfloat16 [768, 768], replicated, may hold values from -0.21875 to 0.21875
- slide_bias: float32 [768], replicated, may hold values from -2 to 2
- cotangent: float32 [8, 768], P('dp'), may hold values from -180 to 180
Outputs:
- tile_out: bfloat16 [512, 16, 16, 384], P(('dp', 'group'))
- slide_feature: float32 [8, 768], P('dp')
- grad_expand: float32 [589824], P(('dp', 'group'))
- grad_reduce: float32 [589824], P(('dp', 'group'))
- grad_depth: float32 [18816], P(('dp', 'group'))
Inputs may be any that keep to these rules, and one draw needn't show every extreme that they name: counts[d] is the number of tiles of slide d. At each group index the present tiles of all slides number at most 32, at group index 0 exactly that. routing[d, g, s] is -1 where the slot holds no tile, else e * 4 + p: the tile is processed at slot p of the device with dp index e and group index g. Each processing slot receives at most one tile; at group index 0 every one receives a tile. A device sends at most 1 tiles to each dp index, and some device sends exactly 1 to each.
All inputs are finite; a program needn't handle non-finite values.
Results may differ from a plain program's by a relative error of at most 0.013.
Values may be sent and summed in bfloat16 or wider, within the bound.
A program may use at most 128 MiB of HBM per device.

v0:
```python
import math
import jax
import jax.numpy as jnp
from jax import lax
from jax.sharding import PartitionSpec as P

E = 768
KS = 7
KERNEL_TAPS = 7
TILE_DILATION = 3
PROC = 4
EPSILON = 1e-06
HALF_ROOT = 0.7071067811865476
INV_ROOT_TAU = 0.3989422804014327


def gelu_exact(values):
    return 0.5 * values * (1.0 + jax.scipy.special.erf(values * HALF_ROOT))


def gelu_slope(values):
    return 0.5 * (
        1.0 + jax.scipy.special.erf(values * HALF_ROOT)
    ) + values * INV_ROOT_TAU * jnp.exp(-0.5 * values * values)


def contract_rows(left_side, right_side):
    return lax.dot_general(
        left_side, right_side, (((0,), (0,)), ((), ())), preferred_element_type=jnp.float32
    )


def contract_cols(left_side, right_side):
    return lax.dot_general(
        left_side, right_side, (((1,), (1,)), ((), ())), preferred_element_type=jnp.float32
    )


def padded_tiles(work_tiles):
    border_width = KS // 2
    return jnp.pad(
        work_tiles, ((0, 0), (border_width, border_width), (border_width, border_width), (0, 0))
    )


def block_forward(
    work_tiles,
    depth_kernel,
    depth_bias,
    norm_gain,
    norm_shift,
    expand_weight,
    expand_bias,
    reduce_weight,
    reduce_bias,
    layer_scale,
    head_weight,
):
    tile_count = work_tiles.shape[0]
    tile_side = work_tiles.shape[1]
    channels = work_tiles.shape[3]
    pixels = tile_side * tile_side
    padded = padded_tiles(work_tiles)
    running = jnp.zeros(work_tiles.shape, jnp.float32) + depth_bias
    for tap_row in range(KS):
        for tap_col in range(KS):
            running = (
                running
                + depth_kernel[tap_row * KS + tap_col]
                * padded[:, tap_row : tap_row + tile_side, tap_col : tap_col + tile_side]
            )
    depth_out = running.reshape(tile_count * pixels, channels)
    chan_mean = jnp.mean(depth_out, axis=1, keepdims=True)
    centred = depth_out - chan_mean
    inv_std = lax.rsqrt(jnp.mean(centred * centred, axis=1, keepdims=True) + EPSILON)
    unit_norm = centred * inv_std
    normed = (unit_norm * norm_gain + norm_shift).astype(jnp.bfloat16)
    pre_act = jnp.dot(normed, expand_weight, preferred_element_type=jnp.float32) + expand_bias
    hidden = gelu_exact(pre_act).astype(jnp.bfloat16)
    mlp_out = jnp.dot(hidden, reduce_weight, preferred_element_type=jnp.float32) + reduce_bias
    section_rows = (
        work_tiles.reshape(tile_count * pixels, channels) + layer_scale * mlp_out
    ).astype(jnp.bfloat16)
    head_pre = jnp.dot(section_rows, head_weight, preferred_element_type=jnp.float32)
    tile_embed = jnp.mean(gelu_exact(head_pre).reshape(tile_count, pixels, -1), axis=1).astype(
        jnp.bfloat16
    )
    return (
        section_rows.reshape(work_tiles.shape),
        tile_embed,
        (unit_norm, inv_std, normed, pre_act, hidden, head_pre),
    )


def block_backward(
    work_tiles,
    saved_acts,
    embed_grad,
    norm_gain,
    expand_weight,
    reduce_weight,
    layer_scale,
    head_weight,
):
    unit_norm, inv_std, normed, pre_act, hidden, head_pre = saved_acts
    tile_count = work_tiles.shape[0]
    tile_side = work_tiles.shape[1]
    channels = work_tiles.shape[3]
    pixels = tile_side * tile_side
    slope_head = gelu_slope(head_pre).reshape(tile_count, pixels, -1)
    grad_head = (embed_grad.astype(jnp.float32)[:, None, :] / float(pixels) * slope_head).astype(
        jnp.bfloat16
    )
    grad_head = grad_head.reshape(tile_count * pixels, -1)
    grad_block = contract_cols(grad_head, head_weight)
    grad_mlp = (layer_scale * grad_block).astype(jnp.bfloat16)
    reduce_grad = contract_rows(hidden, grad_mlp)
    grad_hidden = contract_cols(grad_mlp, reduce_weight)
    grad_pre = (grad_hidden * gelu_slope(pre_act)).astype(jnp.bfloat16)
    expand_grad = contract_rows(normed, grad_pre)
    grad_norm = contract_cols(grad_pre, expand_weight)
    scaled_grad = grad_norm * norm_gain
    grad_depthwise = inv_std * (
        scaled_grad
        - jnp.mean(scaled_grad, axis=1, keepdims=True)
        - unit_norm * jnp.mean(scaled_grad * unit_norm, axis=1, keepdims=True)
    )
    grad_depthwise = grad_depthwise.reshape(tile_count, tile_side, tile_side, channels)
    padded = padded_tiles(work_tiles)
    tap_grads = []
    for tap_row in range(KS):
        for tap_col in range(KS):
            tap_grads.append(
                jnp.sum(
                    grad_depthwise
                    * padded[:, tap_row : tap_row + tile_side, tap_col : tap_col + tile_side],
                    axis=(0, 1, 2),
                )
            )
    return (expand_grad, reduce_grad, jnp.stack(tap_grads))


def position_code(positions):
    half_width = E // 2
    channel_ids = jnp.arange(half_width, dtype=jnp.int32)
    frequency = jnp.exp(
        (2 * (channel_ids // 2)).astype(jnp.float32) * (-math.log(10000.0) / half_width)
    )
    pieces = []
    for coord_axis in range(2):
        angles = positions[coord_axis].astype(jnp.float32)[:, None] * frequency[None, :]
        pieces.append(jnp.where(channel_ids % 2 == 0, jnp.sin(angles), jnp.cos(angles)))
    return jnp.concatenate(pieces, axis=1)


def dilate(seq_float, slide_taps, travel_direction):
    length = seq_float.shape[0]
    border_width = KERNEL_TAPS // 2 * TILE_DILATION
    padded = jnp.pad(seq_float, ((border_width, border_width), (0, 0)))
    running = jnp.zeros(seq_float.shape, jnp.float32)
    for shift_amount in range(KERNEL_TAPS):
        leading_row = (
            border_width + travel_direction * (shift_amount - KERNEL_TAPS // 2) * TILE_DILATION
        )
        running = running + slide_taps[shift_amount] * padded[leading_row : leading_row + length]
    return running


def slide_pass(sequence, seq_present, slide_count, slide_cot, slide_taps, slide_weight, slide_bias):
    seq_float = sequence.astype(jnp.float32)
    mixed = (seq_float + dilate(seq_float, slide_taps, 1)).astype(jnp.bfloat16)
    agg_pre = jnp.dot(mixed, slide_weight, preferred_element_type=jnp.float32) + slide_bias
    weight = seq_present.astype(jnp.float32) / slide_count.astype(jnp.float32)
    feature = jnp.sum(gelu_exact(agg_pre) * weight[:, None], axis=0)
    grad_agg = (slide_cot[None, :] * weight[:, None] * gelu_slope(agg_pre)).astype(jnp.bfloat16)
    grad_mixed = contract_cols(grad_agg, slide_weight)
    seq_grad = (
        (grad_mixed + dilate(grad_mixed, slide_taps, -1)) * seq_present.astype(jnp.float32)[:, None]
    ).astype(jnp.bfloat16)
    return (feature, seq_grad)


def sender_table(my_list, slides, places):
    dest_dev = jnp.where(my_list >= 0, my_list // PROC, -1)
    is_hit = dest_dev[None, :] == jnp.arange(slides, dtype=jnp.int32)[:, None]
    order_rank = jnp.cumsum(is_hit.astype(jnp.int32), axis=1) - 1
    chosen = is_hit[:, None, :] & (
        order_rank[:, None, :] == jnp.arange(places, dtype=jnp.int32)[None, :, None]
    )
    return chosen.reshape(slides * places, -1)


def receiver_table(route_rows, my_slide, places):
    dest_dev = jnp.where(route_rows >= 0, route_rows // PROC, -1)
    is_hit = dest_dev == my_slide
    order_rank = jnp.cumsum(is_hit.astype(jnp.int32), axis=1) - 1
    chosen = is_hit[:, None, :] & (
        order_rank[:, None, :] == jnp.arange(places, dtype=jnp.int32)[None, :, None]
    )
    target = jnp.sum(jnp.where(chosen, (route_rows % PROC)[:, None, :], 0), axis=2).reshape(-1)
    is_used = jnp.any(chosen, axis=2).reshape(-1)
    return (target[None, :] == jnp.arange(PROC, dtype=jnp.int32)[:, None]) & is_used[None, :]


def on_device(
    tile_maps,
    positions,
    counts,
    routing,
    depth_kernel,
    depth_bias,
    norm_gain,
    norm_shift,
    expand_weight,
    expand_bias,
    reduce_weight,
    reduce_bias,
    layer_scale,
    head_weight,
    slide_taps,
    slide_weight,
    slide_bias,
    cotangent,
):
    params = (
        depth_kernel,
        depth_bias,
        norm_gain,
        norm_shift,
        expand_weight,
        expand_bias,
        reduce_weight,
        reduce_bias,
        layer_scale,
        head_weight,
    )
    slides = lax.axis_size("dp")
    members = lax.axis_size("group")
    my_slide = lax.axis_index("dp")
    my_member = lax.axis_index("group")
    slot_count = tile_maps.shape[0]
    embed_width = head_weight.shape[1]
    places = slot_count // slides
    route_rows = routing[:, 0, :]
    my_list = lax.dynamic_index_in_dim(route_rows, my_slide, 0, keepdims=False)
    send_pick = sender_table(my_list, slides, places).astype(jnp.bfloat16)
    take_bool = receiver_table(route_rows, my_slide, places)
    take_pick = take_bool.astype(jnp.bfloat16)
    filled = jnp.any(take_bool, axis=1)
    packed = jnp.dot(
        send_pick, tile_maps.reshape(slot_count, -1), preferred_element_type=jnp.float32
    ).astype(jnp.bfloat16)
    packed = packed.reshape((slides * places,) + tile_maps.shape[1:])
    arrived = lax.all_to_all(packed, "dp", split_axis=0, concat_axis=0, tiled=True)
    work_tiles = jnp.dot(
        take_pick, arrived.reshape(slides * places, -1), preferred_element_type=jnp.float32
    ).astype(jnp.bfloat16)
    work_tiles = work_tiles.reshape((take_pick.shape[0],) + tile_maps.shape[1:])
    section_out, tile_embed, saved_acts = block_forward(work_tiles, *params)
    tile_out = jnp.where(filled[:, None, None, None], section_out, jnp.zeros((), jnp.bfloat16))
    returned = contract_rows(take_pick, tile_embed).astype(jnp.bfloat16)
    came_back = lax.all_to_all(returned, "dp", split_axis=0, concat_axis=0, tiled=True)
    own_emb = contract_rows(send_pick, came_back)
    slide_count = counts[0]
    own_seq = jnp.arange(slot_count, dtype=jnp.int32) * members + my_member
    own_present = own_seq < slide_count
    slide_rows = jnp.where(
        own_present[:, None],
        (own_emb + position_code(positions)).astype(jnp.bfloat16),
        jnp.zeros((), jnp.bfloat16),
    )
    gathered = lax.all_gather(
        slide_rows.reshape(slot_count, 1, embed_width), "group", axis=1, tiled=True
    )
    sequence = gathered.reshape(slot_count * members, embed_width)
    seq_present = jnp.arange(slot_count * members, dtype=jnp.int32) < slide_count
    slide_cot = cotangent[0]
    feature, seq_grad = slide_pass(
        sequence, seq_present, slide_count, slide_cot, slide_taps, slide_weight, slide_bias
    )
    own_grad = lax.dynamic_index_in_dim(
        seq_grad.reshape(slot_count, members, embed_width), my_member, 1, keepdims=False
    )
    outgoing = jnp.dot(send_pick, own_grad, preferred_element_type=jnp.float32).astype(jnp.bfloat16)
    incoming = lax.all_to_all(outgoing, "dp", split_axis=0, concat_axis=0, tiled=True)
    embed_grad = jnp.dot(take_pick, incoming, preferred_element_type=jnp.float32).astype(
        jnp.bfloat16
    )
    source_tiles, _ = lax.optimization_barrier((work_tiles, embed_grad))
    kept_acts = block_forward(source_tiles, *params)[2]
    expand_grad, reduce_grad, depth_grad = block_backward(
        source_tiles,
        kept_acts,
        embed_grad,
        norm_gain,
        expand_weight,
        reduce_weight,
        layer_scale,
        head_weight,
    )
    shares = (
        lax.psum_scatter(expand_grad.reshape(-1), ("dp", "group"), scatter_dimension=0, tiled=True),
        lax.psum_scatter(reduce_grad.reshape(-1), ("dp", "group"), scatter_dimension=0, tiled=True),
        lax.psum_scatter(depth_grad.reshape(-1), ("dp", "group"), scatter_dimension=0, tiled=True),
    )
    return (tile_out, feature[None, :], shares[0], shares[1], shares[2])


def solution(mesh):
    return jax.shard_map(
        on_device,
        mesh=mesh,
        in_specs=(
            P(("dp", "group"), None, None, None),
            P(None, ("dp", "group")),
            P("dp"),
            P(None, "group", None),
            P(),
            P(),
            P(),
            P(),
            P(),
            P(),
            P(),
            P(),
            P(),
            P(),
            P(),
            P(),
            P(),
            P("dp", None),
        ),
        out_specs=(
            P(("dp", "group"), None, None, None),
            P("dp", None),
            P(("dp", "group")),
            P(("dp", "group")),
            P(("dp", "group")),
        ),
        check_vma=False,
    )
```

profile of v0, /device:TPU:1, one launch (start us, length us, event | category | flops | bytes accessed | tf_op | source)
XLA Modules:
  0.0 371.2 jit_solution(15879071314645622072)
XLA Ops:
  7.2 0.8 compare_select_fusion.4
  8.1 2.3 copy.39
  11.0 1.4 copy.32
  12.4 6.1 %all-to-all-start = ((bf16[8,16,16,384]{3,2,1,0:T(8,128)(2,1)}), bf16[8,16,16,384]{3,2,1,0:T(8,128)(2,1)S(1)}, u32[]{:S(2)}, u32[]{:S(2)}) async-start(bf16[8,16,16,384]{3,2,1,0:T(8,128)(2,1)} %copy.32), calls=%async_computation | async-start | bytes 3145728 | tf_op jit(solution)/shard_map/all_to_all | solution.py:254
  18.6 1.4 reduce_window_sum.17
  23.6 0.7 slice_reduce_fusion.54
  24.3 0.7 slice_reduce_fusion.55
  25.6 0.8 fusion.166
  26.4 12.8 %all-to-all-done = bf16[8,16,16,384]{3,2,1,0:T(8,128)(2,1)S(1)} async-done(((bf16[8,16,16,384]{3,2,1,0:T(8,128)(2,1)}), bf16[8,16,16,384]{3,2,1,0:T(8,128)(2,1)S(1)}, u32[]{:S(2)}, u32[]{:S(2)}) %all-to-all-start) | async-done | bytes 1572896 | tf_op jit(solution)/shard_map/all_to_all | solution.py:254
  39.2 0.9 copy.40
  40.7 1.6 reshape.395
  43.3 12.8 %fusion.203 = (f32[4,16,16]{2,1,0:T(8,128)S(1)}, f32[4,16,16,384]{3,2,1,0:T(8,128)S(1)}) fusion(f32[384]{0:T(512)S(1)} %copy-done.11, f32[384]{0:T(512)S(1)} %copy-done.12, f32[384]{0:T(512)S(1)} %copy-done.33, f32[384]{0:T(512)S(1)} %copy-done.34, f32[384]{0:T(512)S(1)} %copy-done.35, f32[384]{0:T(512)S(1)} %copy-done.36, f32[384]{0:T(512)S(1)} %copy-done.37, ...), kind=kLoop, calls=%fused_computation.532 | loop fusion | flops 58194944 | bytes 2440192 | tf_op jit(solution)/shard_map/reduce_sum | solution.py:73
  56.8 1.4 div.79
  58.2 1.1 multiply_reduce_fusion.3
  60.0 1.4 rsqrt.23
  61.4 1.9 fusion.112
  63.4 5.5 %add_convert_fusion.1 = bf16[1024,384]{1,0:T(8,128)(2,1)S(1)} fusion(f32[1024,384]{1,0:T(8,128)} %reshape.395, bf16[1536,384]{1,0:T(8,128)(2,1)} %param.28, bf16[1024,384]{1,0:T(8,128)(2,1)} %fusion.112, bf16[384,1536]{1,0:T(8,128)(2,1)S(1)} %copy-done, f32[1536]{0:T(1024)} %param.27, f32[384]{0:T(512)} %param.29, f32[384]{0:T(512)} %param.30), kind=kOutput, calls=%fused_computation.323 | convolution fusion | flops 2426929152 | bytes 5514240 | tf_op jit(solution)/shard_map/dot_general | solution.py:80
  69.1 1.3 bitcast_reduce_fusion
  72.4 4.1 %all-to-all-start.1 = ((bf16[8,2,384]{2,1,0:T(2,128)(2,1)}), bf16[8,2,384]{2,1,0:T(2,128)(2,1)S(1)}, u32[]{:S(2)}, u32[]{:S(2)}) async-start(bf16[8,2,384]{2,1,0:T(2,128)(2,1)} %reshape.458), calls=%async_computation.1 | async-start | bytes 24576 | tf_op jit(solution)/shard_map/all_to_all | solution.py:262
  76.6 4.6 %all-to-all-done.1 = bf16[8,2,384]{2,1,0:T(2,128)(2,1)S(1)} async-done(((bf16[8,2,384]{2,1,0:T(2,128)(2,1)}), bf16[8,2,384]{2,1,0:T(2,128)(2,1)S(1)}, u32[]{:S(2)}, u32[]{:S(2)}) %all-to-all-start.1) | async-done | bytes 12320 | tf_op jit(solution)/shard_map/all_to_all | solution.py:262
  81.4 19.9 %all-gather = bf16[8,12288]{1,0:T(8,128)(2,1)S(1)} all-gather(bf16[8,768]{1,0:T(8,128)(2,1)S(1)} %fusion.116), channel_id=2, replica_groups=mesh['dp'=8,'group'=16] {'group'}, dimensions={1}, use_global_device_ids=true | all-gather | bytes 208896 | tf_op jit(solution)/shard_map/all_gather | solution.py:272
  101.4 2.6 multiply_reduce_fusion.4
  105.8 12.9 %all_to_all.29 = bf16[8,2,384]{2,1,0:T(2,128)(2,1)S(1)} all-to-all(bf16[8,2,384]{2,1,0:T(2,128)(2,1)S(1)} %reshape.460), channel_id=1, replica_groups=mesh['dp'=8,'group'=16] {'dp'}, dimensions={0} | all-to-all | bytes 24576 | tf_op jit(solution)/shard_map/all_to_all | solution.py:285
  118.7 0.7 convert_multiply_fusion.96
  119.5 13.6 %fusion.199 = (f32[4,16,16]{2,1,0:T(8,128)S(1)}, f32[4,16,16,384]{3,2,1,0:T(8,128)S(1)}) fusion(f32[384]{0:T(512)} %get-tuple-element.105, f32[384]{0:T(512)} %get-tuple-element.106, f32[384]{0:T(512)} %get-tuple-element.59, f32[384]{0:T(512)} %get-tuple-element.60, f32[384]{0:T(512)} %get-tuple-element.61, f32[384]{0:T(512)} %get-tuple-element.62, ...), kind=kLoop, calls=%fused_computation.530 | loop fusion | flops 58194944 | bytes 2440192 | tf_op jit(solution)/shard_map/reduce_sum | solution.py:73
  133.7 0.8 div.87
  134.6 1.1 multiply_reduce_fusion.2
  136.3 0.8 rsqrt.25
  137.9 2.7 multiply_convert_fusion
  140.6 1.8 fusion.107
  142.5 1.8 fusion.9
  144.3 1.0 multiply_convert_fusion.2
  145.3 3.3 fusion.206
  148.6 3.5 fusion.4
  152.0 2.9 fusion.205
  154.9 2.0 fusion.198
  156.9 6.2 %fusion.105 = (f32[384]{0:T(512)S(1)}, f32[384]{0:T(512)}, f32[384]{0:T(512)}, f32[384]{0:T(512)}, f32[384]{0:T(512)}, /*index=5*/f32[384]{0:T(512)}, f32[384]{0...) fusion(bf16[4,16,16,384]{3,2,1,0:T(8,128)(2,1)S(1)} %bitcast.16, ...), kind=kLoop, calls=%fused_computation.306 | loop fusion | flops 23586048 | bytes 5549056 | tf_op jit(solution)/shard_map/reduce_sum | solution.py:134
  163.1 3.2 fusion.104
  166.3 4.4 %fusion.106 = (f32[384]{0:T(512)}, f32[384]{0:T(512)}, f32[384]{0:T(512)}, f32[384]{0:T(512)}, f32[384]{0:T(512)}, /*index=5*/f32[384]{0:T(512)}, f32[384]{0:T(5...) fusion(bf16[4,16,16,384]{3,2,1,0:T(8,128)(2,1)S(1)} %bitcast.16, ...), kind=kLoop, calls=%fused_computation.307 | loop fusion | flops 21226752 | bytes 2386944 | tf_op jit(solution)/shard_map/reduce_sum | solution.py:134
  170.7 3.3 reshape.391
  174.0 1.5 reshape.392
  189.7 0.7 stack.171
  206.7 1.1 copy-done.3
  207.8 1.0 broadcast_select_fusion
  209.4 150.8 %all-reduce.10.cloned.1.call-done = (f32[589824]{0:T(1024)}, f32[589824]{0:T(1024)}, f32[18816]{0:T(1024)}) async-done(((f32[589824]{0:T(1024)}, f32[589824]{0:T(1024)}, f32[18816]{0:T(1024)}), (f32[589824]{0:T(1024)}, f32[589824]{0:T(1024)}, f32[18816]{0:T(1024)})) %all-reduce.10.cloned.1.call-update) | async-done | bytes 4793872
  360.2 1.4 dynamic-slice.1
  361.6 1.4 dynamic-slice.2
  363.0 1.3 dynamic-slice.3
  (247 shorter events, 43.9 us)
Async XLA Ops:
  7.2 56.2 %copy-start = (bf16[384,1536]{1,0:T(8,128)(2,1)S(1)}, bf16[384,1536]{1,0:T(8,128)(2,1)}, u32[]{:S(2)}) copy-start(bf16[384,1536]{1,0:T(8,128)(2,1)} %param.26) | copy-start | bytes 3538948
  8.1 2.3 copy-start.55
  12.4 6.1 %copy-start.64 = (s32[8,1,8]{2,1,0:T(1,128)S(1)}, s32[8,1,8]{2,1,0:T(1,128)}, u32[]{:S(2)}) copy-start(s32[8,1,8]{2,1,0:T(1,128)} %param.21) | copy-start | bytes 772
  12.4 9.9 %copy-start.4 = (f32[49,384]{1,0:T(8,128)S(1)}, f32[49,384]{1,0:T(8,128)}, u32[]{:S(2)}) copy-start(f32[49,384]{1,0:T(8,128)} %param.22) | copy-start | bytes 225796
  12.4 10.5 %copy-start.5 = (f32[7,768]{1,0:T(8,128)S(1)}, f32[7,768]{1,0:T(8,128)}, u32[]{:S(2)}) copy-start(f32[7,768]{1,0:T(8,128)} %param.32) | copy-start | bytes 64516
  12.4 13.2 %copy-start.67 = (s32[2,8]{1,0:T(2,128)S(1)}, s32[2,8]{1,0:T(2,128)}, u32[]{:S(2)}) copy-start(s32[2,8]{1,0:T(2,128)} %param.19) | copy-start | bytes 196
  12.4 26.8 %all-to-all-start = ((bf16[8,16,16,384]{3,2,1,0:T(8,128)(2,1)}), bf16[8,16,16,384]{3,2,1,0:T(8,128)(2,1)S(1)}, u32[]{:S(2)}, u32[]{:S(2)}) async-start(bf16[8,16,16,384]{3,2,1,0:T(8,128)(2,1)} %copy.32), calls=%async_computation | async-start | bytes 3145728 | tf_op jit(solution)/shard_map/all_to_all | solution.py:254
  25.6 14.5 %copy-start.61 = (pred[4,8]{1,0:T(4,128)(4,1)}, pred[4,8]{1,0:T(4,128)(4,1)S(1)}, u32[]{:S(2)}) copy-start(pred[4,8]{1,0:T(4,128)(4,1)S(1)} %get-tuple-element.121) | copy-start | bytes 100
  42.3 0.7 copy-start.8
  42.3 0.7 copy-start.9
  42.3 0.7 copy-start.10
  42.4 0.7 copy-start.19
  42.5 0.7 copy-start.33
  42.6 0.7 copy-start.34
  42.6 0.7 copy-start.35
  63.4 5.5 %copy-start.71 = (bf16[384,768]{1,0:T(8,128)(2,1)S(1)}, bf16[384,768]{1,0:T(8,128)(2,1)}, u32[]{:S(2)}) copy-start(bf16[384,768]{1,0:T(8,128)(2,1)} %param.31) | copy-start | bytes 1769476
  68.9 1.5 copy-start.2
  68.9 1.5 copy-start.62
  68.9 7.6 %copy-start.65 = (f32[1,768]{1,0:T(1,128)S(1)}, f32[1,768]{1,0:T(1,128)}, u32[]{:S(2)}) copy-start(f32[1,768]{1,0:T(1,128)} %param.35) | copy-start | bytes 9220
  68.9 12.3 %copy-start.52 = (f32[8,384]{1,0:T(8,128)S(1)}, f32[8,384]{1,0:T(8,128)}, u32[]{:S(2)}) copy-start(f32[8,384]{1,0:T(8,128)} %get-tuple-element.129) | copy-start | bytes 36868
  68.9 12.3 %copy-start.53 = (f32[8,384]{1,0:T(8,128)S(1)}, f32[8,384]{1,0:T(8,128)}, u32[]{:S(2)}) copy-start(f32[8,384]{1,0:T(8,128)} %get-tuple-element.130) | copy-start | bytes 36868
  69.0 12.3 %copy-start.56 = (pred[8,8]{1,0:T(8,128)(4,1)S(1)}, pred[8,8]{1,0:T(8,128)(4,1)}, u32[]{:S(2)}) copy-start(pred[8,8]{1,0:T(8,128)(4,1)} %copy-done.55) | copy-start | bytes 196
  69.0 32.4 %copy-start.45 = (f32[768]{0:T(1024)S(1)}, f32[768]{0:T(1024)}, u32[]{:S(2)}) copy-start(f32[768]{0:T(1024)} %get-tuple-element.107) | copy-start | bytes 9220
  69.0 32.4 %copy-start.46 = (f32[768]{0:T(1024)S(1)}, f32[768]{0:T(1024)}, u32[]{:S(2)}) copy-start(f32[768]{0:T(1024)} %get-tuple-element.108) | copy-start | bytes 9220
  69.0 32.4 %copy-start.47 = (f32[768]{0:T(1024)S(1)}, f32[768]{0:T(1024)}, u32[]{:S(2)}) copy-start(f32[768]{0:T(1024)} %get-tuple-element.109) | copy-start | bytes 9220
  69.0 32.4 %copy-start.48 = (f32[768]{0:T(1024)S(1)}, f32[768]{0:T(1024)}, u32[]{:S(2)}) copy-start(f32[768]{0:T(1024)} %get-tuple-element.110) | copy-start | bytes 9220
  69.0 32.4 %copy-start.49 = (f32[768]{0:T(1024)S(1)}, f32[768]{0:T(1024)}, u32[]{:S(2)}) copy-start(f32[768]{0:T(1024)} %get-tuple-element.111) | copy-start | bytes 9220
  69.0 32.4 %copy-start.50 = (f32[768]{0:T(1024)S(1)}, f32[768]{0:T(1024)}, u32[]{:S(2)}) copy-start(f32[768]{0:T(1024)} %get-tuple-element.112) | copy-start | bytes 9220
  69.0 32.4 %copy-start.51 = (f32[768]{0:T(1024)S(1)}, f32[768]{0:T(1024)}, u32[]{:S(2)}) copy-start(f32[768]{0:T(1024)} %get-tuple-element.113) | copy-start | bytes 9220
  69.0 32.4 %copy-start.74 = (f32[768]{0:T(1024)S(1)}, f32[768]{0:T(1024)}, u32[]{:S(2)}) copy-start(f32[768]{0:T(1024)} %param.34) | copy-start | bytes 9220
  69.0 32.4 %copy-start.77 = (f32[128]{0:T(128)S(1)}, f32[128]{0:T(128)}, u32[]{:S(2)}) copy-start(f32[128]{0:T(128)} %compare_select_fusion.8) | copy-start | bytes 1540
  72.4 8.8 %all-to-all-start.1 = ((bf16[8,2,384]{2,1,0:T(2,128)(2,1)}), bf16[8,2,384]{2,1,0:T(2,128)(2,1)S(1)}, u32[]{:S(2)}, u32[]{:S(2)}) async-start(bf16[8,2,384]{2,1,0:T(2,128)(2,1)} %reshape.458), calls=%async_computation.1 | async-start | bytes 24576 | tf_op jit(solution)/shard_map/all_to_all | solution.py:262
  76.5 283.7 %all-reduce.10.cloned.1.call-start = ((), (), s32[]{:S(2)}) async-start(), calls=%async_computation.3 | async-start | bytes 9592832
  101.4 2.6 copy-start.69
  133.1 4.1 %copy-start.57 = (f32[384]{0:T(512)S(1)}, f32[384]{0:T(512)}, u32[]{:S(2)}) copy-start(f32[384]{0:T(512)} %param.25) | copy-start | bytes 4612
  133.1 4.0 %copy-start.58 = (f32[384]{0:T(512)S(1)}, f32[384]{0:T(512)}, u32[]{:S(2)}) copy-start(f32[384]{0:T(512)} %param.24) | copy-start | bytes 4612
  137.2 0.7 copy-start.73
  137.9 2.7 copy-start.70
  137.9 2.7 copy-start.75
  137.9 2.7 copy-start.76
  140.6 1.9 copy-start.54
  140.6 1.9 copy-start.72
  170.7 3.3 copy-start.1
  174.0 23.1 %copy-start.60 = (f32[384]{0:T(512)S(1)}, f32[384]{0:T(512)}, u32[]{:S(2)}) copy-start(f32[384]{0:T(512)} %get-tuple-element.40) | copy-start | bytes 4612
  174.0 23.1 %copy-start.59 = (f32[384]{0:T(512)S(1)}, f32[384]{0:T(512)}, u32[]{:S(2)}) copy-start(f32[384]{0:T(512)} %get-tuple-element.41) | copy-start | bytes 4612
  206.7 1.1 copy-start.3
  206.7 1.1 copy-start.66
  206.7 2.1 copy-start.63
  (33 other events, 22.4 us)
Sparse Core Ops, SparseCore 0:
  206.8 153.3 all-reduce.9
where the time goes:
time: 373 us; the launch traced here: 371 us
  waiting for transfers between devices  168 us (45%)
  local copies, waits for them, and re-layouts  57.7 us (15%)
  other arithmetic  55.4 us (15%)
  blocking collectives  32.8 us (9%)
  matrix products  31.1 us (8%)
  between operations  15.8 us (4%)
  starting transfers between devices  10.2 us (3%)
    unnamed x2, waiting for transfers between devices  151 us
    another operation x50, local copies, waits for them, and re-layouts, block_backward(): return (expand_grad, reduce_grad, jnp.stack(tap_grads))  30.5 us
    reduce_sum x2, other arithmetic, block_forward(): chan_mean = jnp.mean(depth_out, axis=1, keepdims=True)  26.4 us
    all_gather x1, blocking collectives, on_device(): lax.all_gather(slide_rows.reshape(slot_count, 1, embed_width), 'group', a...  19.9 us
    reduce_sum x3, other arithmetic, block_backward(): jnp.sum(grad_depthwise * padded[:, tap_row:tap_row + tile_side, tap_col:t...  13.8 us
    all_to_all x1, blocking collectives, on_device(): lax.all_to_all(outgoing, 'dp', split_axis=0, concat_axis=0, tiled=True)  12.9 us
    all_to_all x1, waiting for transfers between devices, on_device(): lax.all_to_all(packed, 'dp', split_axis=0, concat_axis=0, tiled=True)  12.8 us
    unnamed x166, local copies, waits for them, and re-layouts  10.3 us
  transfers between devices with their start and end apart: 3, of which 3 were waited for; matrix products, arithmetic and copies ran while one was open for 2% of the time, Pallas kernels for 0%

commit v1 on v0

--- a/solution.py
+++ b/solution.py
@@ -269,8 +269,14 @@
         (own_emb + position_code(positions)).astype(jnp.bfloat16),
         jnp.zeros((), jnp.bfloat16),
     )
-    gathered = lax.all_gather(
-        slide_rows.reshape(slot_count, 1, embed_width), "group", axis=1, tiled=True
+    gathered = jnp.concatenate(
+        lax.all_to_all(
+            jnp.stack([slide_rows.reshape(slot_count, 1, embed_width)] * lax.axis_size("group")),
+            "group",
+            0,
+            0,
+        ),
+        axis=1,
     )
     sequence = gathered.reshape(slot_count * members, embed_width)
     seq_present = jnp.arange(slot_count * members, dtype=jnp.int32) < slide_count

time: 373 us -> 334 us (0.90)
  local copies, waits for them, and re-layouts: 57.7 us -> 29.4 us
  blocking collectives: 32.8 us -> 9.04 us
  starting transfers between devices: 10.2 us -> 17.8 us
  waiting for transfers between devices: 168 us -> 175 us
    another operation x50, local copies, waits for them, and re-layouts: 30.5 us -> 0.35 us  [block_backward(): return (expand_grad, reduce_grad, jnp.stack(tap_grads))]
    all_gather x1 -> x0, blocking collectives: 19.9 us -> none  [on_device(): lax.all_gather(slide_rows.reshape(slot_count, 1, embed_width), 'group', a...]
    all_to_all x0 -> x1, starting transfers between devices: none -> 7.59 us  [on_device(): lax.all_to_all(jnp.stack([slide_rows.reshape(slot_count, 1, embed_width)]...]
    all_to_all x0 -> x1, waiting for transfers between devices: none -> 6.97 us  [on_device(): lax.all_to_all(jnp.stack([slide_rows.reshape(slot_count, 1, embed_width)]...]
    all_to_all x1, blocking collectives: 12.9 us -> 9.04 us  [on_device(): lax.all_to_all(outgoing, 'dp', split_axis=0, concat_axis=0, tiled=True)]
    unnamed x166 -> x176, local copies, waits for them, and re-layouts: 10.3 us -> 10.4 us
  transfers between devices with their start and end apart: 3 -> 4, of which waited for: 3 -> 4; matrix products, arithmetic and copies ran while one was open for 2% -> 2% of each run, Pallas kernels for 0% -> 0%
where the time goes in v1:
time: 334 us; the launch traced here: 332 us
  waiting for transfers between devices  175 us (52%)
  other arithmetic  53.6 us (16%)
  matrix products  31.1 us (9%)
  local copies, waits for them, and re-layouts  29.4 us (9%)
  starting transfers between devices  17.8 us (5%)
  between operations  16.2 us (5%)
  blocking collectives  9.04 us (3%)
    unnamed x2, waiting for transfers between devices  149 us
    reduce_sum x2, other arithmetic, block_forward(): chan_mean = jnp.mean(depth_out, axis=1, keepdims=True)  26.4 us
    all_to_all x1, waiting for transfers between devices, on_device(): lax.all_to_all(packed, 'dp', split_axis=0, concat_axis=0, tiled=True)  14.1 us
    reduce_sum x3, other arithmetic, block_backward(): jnp.sum(grad_depthwise * padded[:, tap_row:tap_row + tile_side, tap_col:t...  12.6 us
    unnamed x176, local copies, waits for them, and re-layouts  10.4 us
    all_to_all x1, blocking collectives, on_device(): lax.all_to_all(outgoing, 'dp', split_axis=0, concat_axis=0, tiled=True)  9.04 us
    all_to_all x1, starting transfers between devices, on_device(): lax.all_to_all(jnp.stack([slide_rows.reshape(slot_count, 1, embed_width)]...  7.59 us
    dot_general x2, matrix products, block_forward(): jnp.dot(hidden, reduce_weight, preferred_element_type=jnp.float32)  7.33 us
  transfers between devices with their start and end apart: 4, of which 4 were waited for; matrix products, arithmetic and copies ran while one was open for 2% of the time, Pallas kernels for 0%

profile of v1, /device:TPU:1, one launch (start us, length us, event | category | flops | bytes accessed | tf_op | source)
XLA Modules:
  0.0 332.3 jit_solution(16169847744508133097)
XLA Ops:
  7.2 0.8 compare_select_fusion.4
  8.1 2.3 copy.42
  11.0 1.4 copy.34
  12.4 6.1 %all-to-all-start = ((bf16[8,16,16,384]{3,2,1,0:T(8,128)(2,1)}), bf16[8,16,16,384]{3,2,1,0:T(8,128)(2,1)S(1)}, u32[]{:S(2)}, u32[]{:S(2)}) async-start(bf16[8,16,16,384]{3,2,1,0:T(8,128)(2,1)} %copy.34), calls=%async_computation | async-start | bytes 3145728 | tf_op jit(solution)/shard_map/all_to_all | solution.py:254
  19.7 1.4 reduce_window_sum.17
  23.0 0.7 slice_reduce_fusion.55
  24.4 0.8 fusion.166
  25.1 14.1 %all-to-all-done = bf16[8,16,16,384]{3,2,1,0:T(8,128)(2,1)S(1)} async-done(((bf16[8,16,16,384]{3,2,1,0:T(8,128)(2,1)}), bf16[8,16,16,384]{3,2,1,0:T(8,128)(2,1)S(1)}, u32[]{:S(2)}, u32[]{:S(2)}) %all-to-all-start) | async-done | bytes 1572896 | tf_op jit(solution)/shard_map/all_to_all | solution.py:254
  39.2 0.9 copy.43
  40.7 1.6 reshape.393
  43.3 12.8 %fusion.203 = (f32[4,16,16]{2,1,0:T(8,128)S(1)}, f32[4,16,16,384]{3,2,1,0:T(8,128)S(1)}) fusion(f32[384]{0:T(512)S(1)} %copy-done.10, f32[384]{0:T(512)S(1)} %copy-done.11, f32[384]{0:T(512)S(1)} %copy-done.32, f32[384]{0:T(512)S(1)} %copy-done.33, f32[384]{0:T(512)S(1)} %copy-done.34, f32[384]{0:T(512)S(1)} %copy-done.35, f32[384]{0:T(512)S(1)} %copy-done.36, ...), kind=kLoop, calls=%fused_computation.533 | loop fusion | flops 58194944 | bytes 2440192 | tf_op jit(solution)/shard_map/reduce_sum | solution.py:73
  56.8 1.4 div.79
  58.2 1.1 multiply_reduce_fusion.3
  60.0 1.4 rsqrt.23
  61.4 2.0 fusion.112
  63.4 5.5 %add_convert_fusion.1 = bf16[1024,384]{1,0:T(8,128)(2,1)S(1)} fusion(f32[1024,384]{1,0:T(8,128)} %reshape.393, bf16[1536,384]{1,0:T(8,128)(2,1)} %param.28, bf16[1024,384]{1,0:T(8,128)(2,1)} %fusion.112, bf16[384,1536]{1,0:T(8,128)(2,1)S(1)} %copy-done, f32[1536]{0:T(1024)} %param.27, f32[384]{0:T(512)} %param.29, f32[384]{0:T(512)} %param.30), kind=kOutput, calls=%fused_computation.323 | convolution fusion | flops 2426929152 | bytes 5514240 | tf_op jit(solution)/shard_map/dot_general | solution.py:80
  69.0 1.3 bitcast_reduce_fusion
  72.3 4.1 %all-to-all-start.1 = ((bf16[8,2,384]{2,1,0:T(2,128)(2,1)}), bf16[8,2,384]{2,1,0:T(2,128)(2,1)S(1)}, u32[]{:S(2)}, u32[]{:S(2)}) async-start(bf16[8,2,384]{2,1,0:T(2,128)(2,1)} %reshape.453), calls=%async_computation.1 | async-start | bytes 24576 | tf_op jit(solution)/shard_map/all_to_all | solution.py:262
  76.5 4.6 %all-to-all-done.1 = bf16[8,2,384]{2,1,0:T(2,128)(2,1)S(1)} async-done(((bf16[8,2,384]{2,1,0:T(2,128)(2,1)}), bf16[8,2,384]{2,1,0:T(2,128)(2,1)S(1)}, u32[]{:S(2)}, u32[]{:S(2)}) %all-to-all-start.1) | async-done | bytes 12320 | tf_op jit(solution)/shard_map/all_to_all | solution.py:262
  81.3 0.7 stack.153
  82.0 7.6 %all-to-all-start.2 = ((bf16[16,8,1,768]{3,1,2,0:T(8,128)(2,1)}), bf16[16,8,1,768]{3,1,2,0:T(8,128)(2,1)S(1)}, u32[]{:S(2)}, u32[]{:S(2)}) async-start(bf16[16,8,1,768]{3,1,2,0:T(8,128)(2,1)} %stack.153), calls=%async_computation.2 | async-start | bytes 393216 | tf_op jit(solution)/shard_map/all_to_all | solution.py:273
  89.8 7.0 %all-to-all-done.2 = bf16[16,8,1,768]{3,1,2,0:T(8,128)(2,1)S(1)} async-done(((bf16[16,8,1,768]{3,1,2,0:T(8,128)(2,1)}), bf16[16,8,1,768]{3,1,2,0:T(8,128)(2,1)S(1)}, u32[]{:S(2)}, u32[]{:S(2)}) %all-to-all-start.2) | async-done | bytes 196640 | tf_op jit(solution)/shard_map/all_to_all | solution.py:273
  96.9 2.6 multiply_reduce_fusion.4
  101.3 9.0 %all_to_all.34 = bf16[8,2,384]{2,1,0:T(2,128)(2,1)S(1)} all-to-all(bf16[8,2,384]{2,1,0:T(2,128)(2,1)S(1)} %reshape.455), channel_id=1, replica_groups=mesh['dp'=8,'group'=16] {'dp'}, dimensions={0} | all-to-all | bytes 24576 | tf_op jit(solution)/shard_map/all_to_all | solution.py:291
  110.4 0.7 convert_multiply_fusion.96
  111.1 13.6 %fusion.199 = (f32[4,16,16]{2,1,0:T(8,128)S(1)}, f32[4,16,16,384]{3,2,1,0:T(8,128)S(1)}) fusion(f32[384]{0:T(512)} %get-tuple-element.105, f32[384]{0:T(512)} %get-tuple-element.106, f32[384]{0:T(512)} %get-tuple-element.59, f32[384]{0:T(512)} %get-tuple-element.60, f32[384]{0:T(512)} %get-tuple-element.61, f32[384]{0:T(512)} %get-tuple-element.62, ...), kind=kLoop, calls=%fused_computation.531 | loop fusion | flops 58194944 | bytes 2440192 | tf_op jit(solution)/shard_map/reduce_sum | solution.py:73
  125.4 0.8 div.87
  126.2 1.1 multiply_reduce_fusion.2
  127.9 0.8 rsqrt.25
  129.5 2.7 multiply_convert_fusion
  132.2 1.8 fusion.107
  134.1 1.8 fusion.9
  135.9 1.0 multiply_convert_fusion.2
  136.9 3.3 fusion.206
  140.2 3.4 %fusion.4 = bf16[1024,1536]{1,0:T(8,128)(2,1)S(1)} fusion(f32[1024,1536]{1,0:T(8,128)S(1)} %get-tuple-element.136, bf16[1024,384]{1,0:T(8,128)(2,1)S(1)} %multiply_convert_fusion.2, bf16[1536,384]{1,0:T(8,128)(2,1)S(1)} %copy-done.76, f32[1536]{0:T(1024)S(1)} %copy-done.79), kind=kOutput, calls=%fused_computation.103 | convolution fusion | flops 1225261056 | bytes 11409408 | tf_op jit(solution)/shard_map/dot_general | solution.py:34
  143.7 2.8 fusion.205
  146.5 2.0 fusion.198
  148.5 6.2 %fusion.105 = (f32[384]{0:T(512)S(1)}, f32[384]{0:T(512)}, f32[384]{0:T(512)}, f32[384]{0:T(512)}, f32[384]{0:T(512)}, /*index=5*/f32[384]{0:T(512)}, f32[384]{0...) fusion(bf16[4,16,16,384]{3,2,1,0:T(8,128)(2,1)S(1)} %bitcast.16, ...), kind=kLoop, calls=%fused_computation.306 | loop fusion | flops 23586048 | bytes 5549056 | tf_op jit(solution)/shard_map/reduce_sum | solution.py:134
  154.7 2.6 fusion.104
  157.3 3.8 %fusion.106 = (f32[384]{0:T(512)S(1)}, f32[384]{0:T(512)S(1)}, f32[384]{0:T(512)S(1)}, f32[384]{0:T(512)S(1)}, f32[384]{0:T(512)S(1)}, /*index=5*/f32[384]{0:T(5...) fusion(bf16[4,16,16,384]{3,2,1,0:T(8,128)(2,1)S(1)} %bitcast.16, ...), kind=kLoop, calls=%fused_computation.307 | loop fusion | flops 21226752 | bytes 2386944 | tf_op jit(solution)/shard_map/reduce_sum | solution.py:134
  161.1 3.2 reshape.389
  164.4 3.2 reshape.390
  169.1 1.1 copy-done.2
  170.2 1.0 broadcast_select_fusion
  171.8 149.4 %all-reduce.10.cloned.1.call-done = (f32[589824]{0:T(1024)}, f32[589824]{0:T(1024)}, f32[18816]{0:T(1024)}) async-done(((f32[589824]{0:T(1024)}, f32[589824]{0:T(1024)}, f32[18816]{0:T(1024)}), (f32[589824]{0:T(1024)}, f32[589824]{0:T(1024)}, f32[18816]{0:T(1024)})) %all-reduce.10.cloned.1.call-update) | async-done | bytes 4793872
  321.3 1.4 dynamic-slice.1
  322.7 1.4 dynamic-slice.2
  324.1 1.3 dynamic-slice.3
  (260 shorter events, 14.2 us)
Async XLA Ops:
  7.2 56.2 %copy-start = (bf16[384,1536]{1,0:T(8,128)(2,1)S(1)}, bf16[384,1536]{1,0:T(8,128)(2,1)}, u32[]{:S(2)}) copy-start(bf16[384,1536]{1,0:T(8,128)(2,1)} %param.26) | copy-start | bytes 3538948
  8.1 2.3 copy-start.47
  12.4 6.1 %copy-start.70 = (s32[8,1,8]{2,1,0:T(1,128)S(1)}, s32[8,1,8]{2,1,0:T(1,128)}, u32[]{:S(2)}) copy-start(s32[8,1,8]{2,1,0:T(1,128)} %param.21) | copy-start | bytes 772
  12.4 9.3 %copy-start.3 = (f32[49,384]{1,0:T(8,128)S(1)}, f32[49,384]{1,0:T(8,128)}, u32[]{:S(2)}) copy-start(f32[49,384]{1,0:T(8,128)} %param.22) | copy-start | bytes 225796
  12.4 12.0 %copy-start.73 = (s32[2,8]{1,0:T(2,128)S(1)}, s32[2,8]{1,0:T(2,128)}, u32[]{:S(2)}) copy-start(s32[2,8]{1,0:T(2,128)} %param.19) | copy-start | bytes 196
  12.4 26.8 %all-to-all-start = ((bf16[8,16,16,384]{3,2,1,0:T(8,128)(2,1)}), bf16[8,16,16,384]{3,2,1,0:T(8,128)(2,1)S(1)}, u32[]{:S(2)}, u32[]{:S(2)}) async-start(bf16[8,16,16,384]{3,2,1,0:T(8,128)(2,1)} %copy.34), calls=%async_computation | async-start | bytes 3145728 | tf_op jit(solution)/shard_map/all_to_all | solution.py:254
  24.4 15.8 %copy-start.67 = (pred[4,8]{1,0:T(4,128)(4,1)}, pred[4,8]{1,0:T(4,128)(4,1)S(1)}, u32[]{:S(2)}) copy-start(pred[4,8]{1,0:T(4,128)(4,1)S(1)} %get-tuple-element.121) | copy-start | bytes 100
  42.6 0.7 copy-start.39
  42.6 0.7 copy-start.40
  63.4 5.5 %copy-start.77 = (bf16[384,768]{1,0:T(8,128)(2,1)S(1)}, bf16[384,768]{1,0:T(8,128)(2,1)}, u32[]{:S(2)}) copy-start(bf16[384,768]{1,0:T(8,128)(2,1)} %param.31) | copy-start | bytes 1769476
  68.9 1.4 copy-start.1
  68.9 1.4 copy-start.68
  68.9 7.6 %copy-start.71 = (f32[1,768]{1,0:T(1,128)S(1)}, f32[1,768]{1,0:T(1,128)}, u32[]{:S(2)}) copy-start(f32[1,768]{1,0:T(1,128)} %param.35) | copy-start | bytes 9220
  68.9 12.2 %copy-start.44 = (f32[8,384]{1,0:T(8,128)S(1)}, f32[8,384]{1,0:T(8,128)}, u32[]{:S(2)}) copy-start(f32[8,384]{1,0:T(8,128)} %get-tuple-element.129) | copy-start | bytes 36868
  68.9 12.2 %copy-start.45 = (f32[8,384]{1,0:T(8,128)S(1)}, f32[8,384]{1,0:T(8,128)}, u32[]{:S(2)}) copy-start(f32[8,384]{1,0:T(8,128)} %get-tuple-element.130) | copy-start | bytes 36868
  68.9 12.2 %copy-start.48 = (pred[8,8]{1,0:T(8,128)(4,1)S(1)}, pred[8,8]{1,0:T(8,128)(4,1)}, u32[]{:S(2)}) copy-start(pred[8,8]{1,0:T(8,128)(4,1)} %copy-done.47) | copy-start | bytes 196
  69.0 20.7 %copy-start.4 = (f32[7,768]{1,0:T(8,128)S(1)}, f32[7,768]{1,0:T(8,128)}, u32[]{:S(2)}) copy-start(f32[7,768]{1,0:T(8,128)} %param.32) | copy-start | bytes 64516
  70.3 26.6 %copy-start.80 = (f32[768]{0:T(1024)S(1)}, f32[768]{0:T(1024)}, u32[]{:S(2)}) copy-start(f32[768]{0:T(1024)} %param.34) | copy-start | bytes 9220
  72.3 8.8 %all-to-all-start.1 = ((bf16[8,2,384]{2,1,0:T(2,128)(2,1)}), bf16[8,2,384]{2,1,0:T(2,128)(2,1)S(1)}, u32[]{:S(2)}, u32[]{:S(2)}) async-start(bf16[8,2,384]{2,1,0:T(2,128)(2,1)} %reshape.453), calls=%async_computation.1 | async-start | bytes 24576 | tf_op jit(solution)/shard_map/all_to_all | solution.py:262
  82.0 14.7 %all-to-all-start.2 = ((bf16[16,8,1,768]{3,1,2,0:T(8,128)(2,1)}), bf16[16,8,1,768]{3,1,2,0:T(8,128)(2,1)S(1)}, u32[]{:S(2)}, u32[]{:S(2)}) async-start(bf16[16,8,1,768]{3,1,2,0:T(8,128)(2,1)} %stack.153), calls=%async_computation.2 | async-start | bytes 393216 | tf_op jit(solution)/shard_map/all_to_all | solution.py:273
  89.6 231.6 %all-reduce.10.cloned.1.call-start = ((), (), s32[]{:S(2)}) async-start(), calls=%async_computation.4 | async-start | bytes 9592832
  96.9 2.6 copy-start.75
  124.7 4.1 %copy-start.49 = (f32[384]{0:T(512)S(1)}, f32[384]{0:T(512)}, u32[]{:S(2)}) copy-start(f32[384]{0:T(512)} %param.25) | copy-start | bytes 4612
  124.7 4.0 %copy-start.50 = (f32[384]{0:T(512)S(1)}, f32[384]{0:T(512)}, u32[]{:S(2)}) copy-start(f32[384]{0:T(512)} %param.24) | copy-start | bytes 4612
  129.5 2.7 copy-start.76
  129.5 2.7 copy-start.81
  129.5 2.7 copy-start.82
  132.2 1.9 copy-start.46
  132.2 1.9 copy-start.78
  164.2 3.5 %copy-start.66 = (f32[384]{0:T(512)S(1)}, f32[384]{0:T(512)}, u32[]{:S(2)}) copy-start(f32[384]{0:T(512)} %get-tuple-element.26) | copy-start | bytes 4612
  164.2 3.6 %copy-start.65 = (f32[384]{0:T(512)S(1)}, f32[384]{0:T(512)}, u32[]{:S(2)}) copy-start(f32[384]{0:T(512)} %get-tuple-element.27) | copy-start | bytes 4612
  164.2 3.6 %copy-start.64 = (f32[384]{0:T(512)S(1)}, f32[384]{0:T(512)}, u32[]{:S(2)}) copy-start(f32[384]{0:T(512)} %get-tuple-element.28) | copy-start | bytes 4612
  164.2 3.6 %copy-start.63 = (f32[384]{0:T(512)S(1)}, f32[384]{0:T(512)}, u32[]{:S(2)}) copy-start(f32[384]{0:T(512)} %get-tuple-element.29) | copy-start | bytes 4612
  164.2 3.6 %copy-start.62 = (f32[384]{0:T(512)S(1)}, f32[384]{0:T(512)}, u32[]{:S(2)}) copy-start(f32[384]{0:T(512)} %get-tuple-element.30) | copy-start | bytes 4612
  164.2 3.6 %copy-start.61 = (f32[384]{0:T(512)S(1)}, f32[384]{0:T(512)}, u32[]{:S(2)}) copy-start(f32[384]{0:T(512)} %get-tuple-element.31) | copy-start | bytes 4612
  164.3 3.6 %copy-start.60 = (f32[384]{0:T(512)S(1)}, f32[384]{0:T(512)}, u32[]{:S(2)}) copy-start(f32[384]{0:T(512)} %get-tuple-element.32) | copy-start | bytes 4612
  164.3 3.7 %copy-start.59 = (f32[384]{0:T(512)S(1)}, f32[384]{0:T(512)}, u32[]{:S(2)}) copy-start(f32[384]{0:T(512)} %get-tuple-element.33) | copy-start | bytes 4612
  164.3 3.7 %copy-start.58 = (f32[384]{0:T(512)S(1)}, f32[384]{0:T(512)}, u32[]{:S(2)}) copy-start(f32[384]{0:T(512)} %get-tuple-element.34) | copy-start | bytes 4612
  164.3 3.7 %copy-start.57 = (f32[384]{0:T(512)S(1)}, f32[384]{0:T(512)}, u32[]{:S(2)}) copy-start(f32[384]{0:T(512)} %get-tuple-element.35) | copy-start | bytes 4612
  164.3 3.7 %copy-start.56 = (f32[384]{0:T(512)S(1)}, f32[384]{0:T(512)}, u32[]{:S(2)}) copy-start(f32[384]{0:T(512)} %get-tuple-element.36) | copy-start | bytes 4612
  164.3 3.7 %copy-start.55 = (f32[384]{0:T(512)S(1)}, f32[384]{0:T(512)}, u32[]{:S(2)}) copy-start(f32[384]{0:T(512)} %get-tuple-element.37) | copy-start | bytes 4612
  164.3 3.7 %copy-start.54 = (f32[384]{0:T(512)S(1)}, f32[384]{0:T(512)}, u32[]{:S(2)}) copy-start(f32[384]{0:T(512)} %get-tuple-element.38) | copy-start | bytes 4612
  164.3 3.7 %copy-start.53 = (f32[384]{0:T(512)S(1)}, f32[384]{0:T(512)}, u32[]{:S(2)}) copy-start(f32[384]{0:T(512)} %get-tuple-element.39) | copy-start | bytes 4612
  164.3 3.7 %copy-start.52 = (f32[384]{0:T(512)S(1)}, f32[384]{0:T(512)}, u32[]{:S(2)}) copy-start(f32[384]{0:T(512)} %get-tuple-element.40) | copy-start | bytes 4612
  164.3 3.7 %copy-start.51 = (f32[384]{0:T(512)S(1)}, f32[384]{0:T(512)}, u32[]{:S(2)}) copy-start(f32[384]{0:T(512)} %get-tuple-element.41) | copy-start | bytes 4612
  169.1 1.1 copy-start.2
  169.1 1.1 copy-start.72
  169.1 2.1 copy-start.69
  (39 other events, 26.6 us)
Sparse Core Ops, SparseCore 0:
  169.2 151.9 all-reduce.9
